TPU v7x, 256 devices: a whole 4x4x8 slice. The times are simulated.
256 devices in a mesh: row: 16 (over x_lo, z), col: 16 (over x_hi, y, core).
Axes of the slice: x: 4 (x_hi: 2, x_lo: 2; x = x_hi * 2 + x_lo), y: 4, z: 8, core: 2. Of those that a mesh axis runs over, the one named last changes fastest.
Arguments:
- counts: int32 [16], replicated, may hold values from 32 to 128, as said below
- cotangent: bfloat16 [2048, 16384], P('col', 'row'), may hold values from -1.1953125 to 1.1953125
- saved_gate: bfloat16 [2048, 26624], P('row', 'col'), may hold values from -9 to 9
- saved_up: bfloat16 [2048, 26624], P('row', 'col'), may hold values from -6 to 6
- down_weight: bfloat16 [26624, 16384], P('col', 'row'), may hold values from -0.0390625 to 0.0390625
Outputs:
- grad_gate: bfloat16 [2048, 26624], P('row', 'col')
- grad_up: bfloat16 [2048, 26624], P('row', 'col')
- grad_down: bfloat16 [26624, 16384], P('col', 'row')
Inputs may be any that keep to these rules, and one draw needn't show every extreme that they name: `counts`: each count is a multiple of 32; in every draw some group has 128 live tokens and another only 32.
All inputs are finite; a program needn't handle non-finite values.
Results may differ from a plain program's by a relative error of at most 0.0049.
Values may be sent and summed in bfloat16 or wider, within the bound.
A program may use at most 128 MiB of HBM per device.

v0:
```python
import jax
import jax.numpy as jnp
from jax import lax
from jax.sharding import PartitionSpec as P


def live_rows(counts, index, tok_dev):
    group = index // tok_dev
    table = jnp.arange(counts.shape[0], dtype=jnp.int32)
    limits = jnp.sum(jnp.where(group[:, None] == table[None, :], counts[None, :], 0), axis=1)
    return index % tok_dev < limits


def activation(gate_piece, up_piece):
    gate_float = gate_piece.astype(jnp.float32)
    up_float = up_piece.astype(jnp.float32)
    sigmoid_gate = jax.nn.sigmoid(gate_float)
    silu_gate = gate_float * sigmoid_gate
    return (gate_float, up_float, sigmoid_gate, silu_gate)


def on_device(counts, cotangent, saved_gate, saved_up, down_weight):
    tok_dev = saved_gate.shape[0]
    local_rows = cotangent.shape[0]
    index = lax.axis_index("col") * local_rows + jnp.arange(local_rows, dtype=jnp.int32)
    live = live_rows(counts, index, tok_dev)
    masked = jnp.where(live[:, None], cotangent, jnp.zeros_like(cotangent))
    grad_rows = lax.all_gather(masked, "col", axis=0, tiled=True)
    picked = grad_rows
    grad_hidden = lax.psum_scatter(
        lax.dot_general(
            picked, down_weight, (((1,), (1,)), ((), ())), preferred_element_type=jnp.float32
        ),
        "row",
        scatter_dimension=0,
        tiled=True,
    )
    gate_float, up_float, sigmoid_gate, silu_gate = activation(saved_gate, saved_up)
    grad_up = (grad_hidden * silu_gate).astype(jnp.bfloat16)
    slope = sigmoid_gate * (1.0 + gate_float * (1.0 - sigmoid_gate))
    grad_gate = (grad_hidden * up_float * slope).astype(jnp.bfloat16)
    hidden = (silu_gate * up_float).astype(jnp.bfloat16)
    picked = grad_rows
    grad_down = lax.dot_general(
        lax.all_gather(hidden, "row", axis=0, tiled=True),
        picked,
        (((0,), (0,)), ((), ())),
        preferred_element_type=jnp.float32,
    )
    return (grad_gate, grad_up, grad_down.astype(jnp.bfloat16))


def solution(mesh):
    return jax.shard_map(
        on_device,
        mesh=mesh,
        in_specs=(P(), P("col", "row"), P("row", "col"), P("row", "col"), P("col", "row")),
        out_specs=(P("row", "col"), P("row", "col"), P("col", "row")),
        check_vma=False,
    )
```

profile of v0, /device:TPU:32, one launch (start us, length us, event | category | flops | bytes accessed | tf_op | source)
XLA Modules:
  0.0 342.1 jit_solution(9932480858162931755)
XLA Ops:
  7.2 0.0 copy-start
  7.2 0.0 all-gather.3.cloned.1.call-start
  7.2 0.9 select_reduce_fusion
  8.2 1.8 broadcast_select_fusion
  10.0 0.0 all-gather.3.cloned.1.call-update
  10.0 0.0 reduce-scatter.2.cloned.1.call-start
  10.0 64.3 %all-gather.3.cloned.1.call-done = bf16[2048,1024]{1,0:T(8,128)(2,1)} async-done(((bf16[128,1024]{1,0:T(8,128)(2,1)}), bf16[2048,1024]{1,0:T(8,128)(2,1)}) %all-gather.3.cloned.1.call-update) | async-done | bytes 4194320 | tf_op jit(solution)/shard_map/all_gather | solution.py:28
  74.3 0.0 copy-done
  74.3 12.4 %fusion.9 = f32[2048,1664]{1,0:T(8,128)} fusion(bf16[2048,1024]{1,0:T(8,128)(2,1)} %all-gather.3.cloned.1.call-done, bf16[1664,1024]{1,0:T(8,128)(2,1)S(1)} %copy-done), kind=kOutput, calls=%fused_computation.25 | convolution fusion | flops 6979321856 | bytes 21233664 | tf_op jit(solution)/shard_map/dot_general | solution.py:31
  86.7 0.0 reduce-scatter.2.cloned.1.call-update
  86.7 0.0 all-gather.5.cloned.1.call-start
  86.8 149.3 %reduce-scatter.2.cloned.1.call-done = f32[128,1664]{1,0:T(8,128)} async-done(((f32[2048,1664]{1,0:T(8,128)}), f32[128,1664]{1,0:T(8,128)}) %reduce-scatter.2.cloned.1.call-update) | async-done | bytes 851984 | tf_op jit(solution)/shard_map/reduce_scatter | solution.py:30
  236.1 2.8 multiply_convert_fusion
  239.0 0.0 all-gather.5.cloned.1.call-update
  239.0 84.3 %all-gather.5.cloned.1.call-done = bf16[2048,1664]{1,0:T(8,128)(2,1)} async-done(((bf16[128,1664]{1,0:T(8,128)(2,1)}), bf16[2048,1664]{1,0:T(8,128)(2,1)}) %all-gather.5.cloned.1.call-update) | async-done | bytes 6815760 | tf_op jit(solution)/shard_map/all_gather | solution.py:45
  323.3 12.2 %convolution_convert_fusion = bf16[1664,1024]{1,0:T(8,128)(2,1)} fusion(bf16[2048,1664]{1,0:T(8,128)(2,1)} %all-gather.5.cloned.1.call-done, bf16[2048,1024]{1,0:T(8,128)(2,1)} %all-gather.3.cloned.1.call-done), kind=kOutput, calls=%fused_computation | convolution fusion | flops 6981025792 | bytes 14417920 | tf_op jit(solution)/shard_map/dot_general | solution.py:44
  (2 shorter events, 0.0 us)
Async XLA Ops:
  7.2 67.1 %copy-start = (bf16[1664,1024]{1,0:T(8,128)(2,1)S(1)}, bf16[1664,1024]{1,0:T(8,128)(2,1)}, u32[]{:S(2)}) copy-start(bf16[1664,1024]{1,0:T(8,128)(2,1)} %param.9) | copy-start | bytes 10223620
  7.2 67.1 %all-gather.3.cloned.1.call-start = ((), (), s32[]{:S(2)}) async-start(), calls=%async_computation.1 | async-start | bytes 4456448 | tf_op jit(solution)/shard_map/all_gather | solution.py:28
  10.0 226.2 %reduce-scatter.2.cloned.1.call-start = ((), (), s32[]{:S(2)}) async-start(), calls=%async_computation.2 | async-start | bytes 14483456 | tf_op jit(solution)/shard_map/reduce_scatter | solution.py:30
  86.7 236.6 %all-gather.5.cloned.1.call-start = ((), (), s32[]{:S(2)}) async-start(), calls=%async_computation.3 | async-start | bytes 7241728 | tf_op jit(solution)/shard_map/all_gather | solution.py:45
Sparse Core Ops, SparseCore 0:
  11.3 62.8 all-gather.2
  86.9 149.2 reduce-scatter.1
  239.1 84.1 all-gather.4
where the time goes:
time: 345 us; the launch traced here: 342 us
  waiting for transfers between devices  298 us (86%)
  matrix products  24.7 us (7%)
  between operations  13.8 us (4%)
  other arithmetic  5.54 us (2%)
    reduce_scatter x1, waiting for transfers between devices, on_device(): lax.psum_scatter(lax.dot_general(picked, down_weight, (((1,), (1,)), ((),...  149 us
    all_gather x1, waiting for transfers between devices, on_device(): lax.all_gather(hidden, 'row', axis=0, tiled=True)  84.3 us
    all_gather x1, waiting for transfers between devices, on_device(): grad_rows = lax.all_gather(masked, 'col', axis=0, tiled=True)  64.3 us
    dot_general x1, matrix products, on_device(): lax.dot_general(picked, down_weight, (((1,), (1,)), ((), ())), preferred_...  12.4 us
    dot_general x1, matrix products, on_device(): lax.dot_general(lax.all_gather(hidden, 'row', axis=0, tiled=True), picked...  12.2 us
  transfers between devices with their start and end apart: 3, of which 3 were waited for; matrix products, arithmetic and copies ran while one was open for 0% of the time, Pallas kernels for 0%

commit v1 on v0

v1 whole, which is shorter than its diff:
```python
import jax
import jax.numpy as jnp
from jax import lax
from jax.experimental import pallas as pl
from jax.experimental.pallas import tpu as pltpu
from jax.sharding import PartitionSpec as P

MESH = pl.DeviceIdType.MESH
GROUPS = 16
TOK = 128
LANES = 128
HOPS = 8
CYCLES = (
    ("zig", 0, 0, 4),
    ("zig", 1, 4, 4),
    ("loop", 0, 8, 1),
    ("loop", 1, 9, 1),
    ("loop", 3, 10, 1),
    ("loop", 4, 11, 1),
    ("loop", 6, 12, 1),
)
TILES = 13
SOURCES = ((0, 0), (1, 0), (0, 1), (0, 3), (0, 2), (1, 1), (1, 3), (1, 2))


def place(cycle, p):
    kind, cut = cycle[:2]
    p = lax.rem(p + 2 * GROUPS, GROUPS)
    if kind == "zig":
        z = p // 2
        x = lax.rem(p + z + cut, 2)
        return x * 8 + z
    x = p // 8
    z = x * (15 - p) + (1 - x) * p
    return x * 8 + lax.rem(z + cut + 1, 8)


def spot(cycle, row):
    kind, cut = cycle[:2]
    x = row // 8
    z = lax.rem(row, 8)
    if kind == "zig":
        return 2 * z + lax.rem(x + z + cut, 2)
    z = lax.rem(z + 15 - cut, 8)
    return x * (15 - z) + (1 - x) * z


def hops_of(i, d):
    return HOPS if (i + d) % 2 == 0 else HOPS - 1


def kernel(
    counts_ref, cot_ref, gate_ref, up_ref, weight_hbm,
    grad_gate_ref, grad_up_ref, grad_down_ref,
    weight, cot, hid, part, stage, arrived,
    weight_sem, cot_send, cot_recv, core_send, core_recv,
    hid_send, hid_recv, sum_send, sum_recv,
):
    row = lax.axis_index("row")
    col = lax.axis_index("col")
    x, z = row // 8, lax.rem(row, 8)
    xh = col // 8
    y = lax.rem(col // 2, 4)
    core = lax.rem(col, 2)

    def at_col(dx, dy, c):
        return lax.rem(xh + dx, 2) * 8 + lax.rem(y + dy, 4) * 2 + c

    load_weight = pltpu.make_async_copy(weight_hbm, weight, weight_sem)
    load_weight.start()

    barrier = pltpu.get_barrier_semaphore()
    rows = [(1 - x) * 8 + z, x * 8 + lax.rem(z + 1, 8), x * 8 + lax.rem(z + 7, 8)]
    cols = [at_col(0, 0, 1 - core)] + [at_col(dx, dy, core) for dx, dy in SOURCES[1:5]]
    for other in rows:
        pl.semaphore_signal(barrier, inc=1, device_id={"row": other}, device_id_type=MESH)
    for other in cols:
        pl.semaphore_signal(barrier, inc=1, device_id={"col": other}, device_id_type=MESH)

    limit = counts_ref[col]
    token = lax.broadcasted_iota(jnp.int32, cot_ref.shape, 0)
    cot[col] = jnp.where(token < limit, cot_ref[...], jnp.zeros_like(cot_ref))
    for t in range(TILES):
        lanes = pl.ds(t * LANES, LANES)
        g = gate_ref[:, lanes].astype(jnp.float32)
        u = up_ref[:, lanes].astype(jnp.float32)
        hid[row, lanes, :] = (g * jax.nn.sigmoid(g) * u).T.astype(jnp.bfloat16)
    pl.semaphore_wait(barrier, len(rows) + len(cols))

    def cot_copy(q):
        dx, dy = SOURCES[q]
        block = cot.at[at_col(dx if dy else 0, 0, core)]
        target = at_col(0, 4 - dy, core) if dy else at_col(1, 0, core)
        return pltpu.make_async_remote_copy(
            src_ref=block, dst_ref=block, send_sem=cot_send.at[q], recv_sem=cot_recv.at[q],
            device_id={"col": target}, device_id_type=MESH,
        )

    def source(q):
        dx = jnp.where((q == 1) | (q > 4), 1, 0)
        dy = jnp.where((q == 2) | (q == 5), 1, 0) + jnp.where((q == 3) | (q == 6), 3, 0)
        dy = dy + jnp.where((q == 4) | (q == 7), 2, 0)
        return dx, dy

    def core_copy(q):
        dx, dy = source(q)
        block = cot.at[at_col(dx, dy, core)]
        return pltpu.make_async_remote_copy(
            src_ref=block, dst_ref=block, send_sem=core_send.at[q], recv_sem=core_recv.at[q],
            device_id={"col": at_col(0, 0, 1 - core)}, device_id_type=MESH,
        )

    def core_arrival(q):
        dx, dy = source(q)
        block = cot.at[at_col(dx, dy, 1 - core)]
        return pltpu.make_async_remote_copy(
            src_ref=block, dst_ref=block, send_sem=core_send.at[q], recv_sem=core_recv.at[q],
            device_id={"col": at_col(0, 0, 1 - core)}, device_id_type=MESH,
        )

    def cot_arrival(q):
        dx, dy = source(q)
        block = cot.at[at_col(dx, dy, core)]
        return pltpu.make_async_remote_copy(
            src_ref=block, dst_ref=block, send_sem=cot_send.at[q], recv_sem=cot_recv.at[q],
            device_id={"col": at_col(0, 0, 1 - core)}, device_id_type=MESH,
        )

    def hid_copy(i, d, s, shift=0):
        cycle = CYCLES[i]
        p = spot(cycle, row)
        way = 1 - 2 * d
        block = hid.at[
            place(cycle, p - way * (s + shift)),
            pl.ds(cycle[2] * LANES, cycle[3] * LANES),
        ]
        return pltpu.make_async_remote_copy(
            src_ref=block, dst_ref=block, send_sem=hid_send.at[i, d, s], recv_sem=hid_recv.at[i, d, s],
            device_id={"row": place(cycle, p + way)}, device_id_type=MESH,
        )

    def sum_copy(i, d, s):
        cycle = CYCLES[i]
        tiles = pl.ds(cycle[2], cycle[3])
        return pltpu.make_async_remote_copy(
            src_ref=stage.at[d, s, tiles], dst_ref=arrived.at[d, s, tiles],
            send_sem=sum_send.at[i, d, s], recv_sem=sum_recv.at[i, d, s],
            device_id={"row": place(cycle, spot(cycle, row) + 1 - 2 * d)}, device_id_type=MESH,
        )

    def each(s, run):
        for i in range(len(CYCLES)):
            for d in range(2):
                if hops_of(i, d) < HOPS:
                    pl.when(s < HOPS - 1)(lambda i=i, d=d: run(i, d))
                else:
                    run(i, d)

    for q in range(1, 5):
        cot_copy(q).start()
    core_copy(0).start()

    def gather_step(s, carry):
        @pl.when(s < HOPS)
        def _():
            def run(i, d):
                @pl.when(s > 0)
                def _():
                    hid_copy(i, d, s - 1, 1).wait_recv()

                hid_copy(i, d, s).start()

            each(s, run)

        @pl.when((s > 0) & (s < HOPS))
        def _():
            cot_arrival(s).wait_recv()
            core_copy(s).start()

        @pl.when(s == 1)
        def _():
            for q in range(5, 8):
                cot_copy(q).start()
            load_weight.wait()

        @pl.when(s > 0)
        def _():
            core_arrival(s - 1).wait_recv()
            dx, dy = source(s - 1)
            first = at_col(dx, dy, 0)
            block = cot[pl.ds(first, 2)].reshape(2 * TOK, cot.shape[2])
            for t in range(0, TILES, 2):
                n = min(2, TILES - t)
                product = lax.dot_general(
                    block, weight[t * LANES:(t + n) * LANES, :], (((1,), (1,)), ((), ())),
                    preferred_element_type=jnp.float32,
                )
                for k in range(n):
                    piece = product[:, k * LANES:(k + 1) * LANES]
                    part[pl.ds(first, 2), t + k] = piece.reshape(2, TOK, LANES)

        return carry

    lax.fori_loop(0, HOPS + 1, gather_step, 0)

    def sum_send_step(s, received):
        def run(i, d):
            cycle = CYCLES[i]
            tiles = pl.ds(cycle[2], cycle[3])
            owner = place(cycle, spot(cycle, row) + (1 - 2 * d) * (hops_of(i, d) - s))
            value = part[owner, tiles]
            if received:
                sum_copy(i, d, s - 1).wait_recv()
                value = value + arrived[d, s - 1, tiles].astype(jnp.float32)
            stage[d, s, tiles] = value.astype(jnp.bfloat16)
            sum_copy(i, d, s).start()

        each(s, run)

    sum_send_step(0, False)
    for i in range(len(CYCLES)):
        for d in range(2):
            hid_copy(i, d, hops_of(i, d) - 1, 1).wait_recv()

    def down(first, n):
        lhs = jnp.concatenate([hid[g, pl.ds(first, n), :] for g in range(GROUPS)], axis=1)
        grad_down_ref[pl.ds(first, n), :] = jnp.dot(
            lhs, cot[...].reshape(GROUPS * TOK, cot.shape[2]), preferred_element_type=jnp.float32
        ).astype(jnp.bfloat16)

    def sum_step(s, carry):
        sum_send_step(s, True)

        @pl.when(s < HOPS - 1)
        def _():
            down(pl.multiple_of((s - 1) * 2 * LANES, 2 * LANES), 2 * LANES)

        return carry

    lax.fori_loop(1, HOPS, sum_step, 0)
    down((TILES - 1) * LANES, LANES)

    for i, (kind, cut, first, count) in enumerate(CYCLES):
        for d in range(2):
            sum_copy(i, d, hops_of(i, d) - 1).wait_recv()
        for t in range(first, first + count):
            lanes = pl.ds(t * LANES, LANES)
            grad = part[row, t]
            for d in range(2):
                grad = grad + arrived[d, hops_of(i, d) - 1, t].astype(jnp.float32)
            g = gate_ref[:, lanes].astype(jnp.float32)
            u = up_ref[:, lanes].astype(jnp.float32)
            sig = jax.nn.sigmoid(g)
            grad_up_ref[:, lanes] = (grad * (g * sig)).astype(jnp.bfloat16)
            slope = sig * (1.0 + g * (1.0 - sig))
            grad_gate_ref[:, lanes] = (grad * u * slope).astype(jnp.bfloat16)

    def drain(s, carry):
        def run(i, d):
            hid_copy(i, d, s).wait_send()
            sum_copy(i, d, s).wait_send()

        each(s, run)
        core_copy(s).wait_send()
        return carry

    lax.fori_loop(0, HOPS, drain, 0)
    for q in range(1, 8):
        cot_copy(q).wait_send()


def on_device(counts, cotangent, saved_gate, saved_up, down_weight):
    tok, ff = saved_gate.shape
    d = cotangent.shape[1]
    vmem = pl.BlockSpec(memory_space=pltpu.VMEM)
    dma = pltpu.SemaphoreType.DMA
    n = len(CYCLES)
    return pl.pallas_call(
        kernel,
        out_shape=(
            jax.ShapeDtypeStruct((tok, ff), jnp.bfloat16),
            jax.ShapeDtypeStruct((tok, ff), jnp.bfloat16),
            jax.ShapeDtypeStruct((ff, d), jnp.bfloat16),
        ),
        in_specs=[
            pl.BlockSpec(memory_space=pltpu.SMEM), vmem, vmem, vmem, pl.BlockSpec(memory_space=pl.ANY),
        ],
        out_specs=(vmem, vmem, vmem),
        scratch_shapes=[
            pltpu.VMEM((ff, d), jnp.bfloat16),
            pltpu.VMEM((GROUPS, tok, d), jnp.bfloat16),
            pltpu.VMEM((GROUPS, ff, tok), jnp.bfloat16),
            pltpu.VMEM((GROUPS, TILES, tok, LANES), jnp.float32),
            pltpu.VMEM((2, HOPS, TILES, tok, LANES), jnp.bfloat16),
            pltpu.VMEM((2, HOPS, TILES, tok, LANES), jnp.bfloat16),
            dma, dma((8,)), dma((8,)), dma((8,)), dma((8,)),
            dma((n, 2, HOPS)), dma((n, 2, HOPS)), dma((n, 2, HOPS)), dma((n, 2, HOPS)),
        ],
        compiler_params=pltpu.CompilerParams(
            collective_id=0, has_side_effects=True, vmem_limit_bytes=60 * 2**20
        ),
        cost_estimate=pl.CostEstimate(
            flops=4 * GROUPS * tok * ff * d, bytes_accessed=4 * ff * d + 8 * tok * ff, transcendentals=2 * tok * ff
        ),
        name="down_backward",
    )(counts, cotangent, saved_gate, saved_up, down_weight)


def solution(mesh):
    return jax.shard_map(
        on_device,
        mesh=mesh,
        in_specs=(P(), P("col", "row"), P("row", "col"), P("row", "col"), P("col", "row")),
        out_specs=(P("row", "col"), P("row", "col"), P("col", "row")),
        check_vma=False,
    )
```

time: 345 us -> 140 us (0.41)
  waiting for transfers between devices: 298 us -> 0 us
  Pallas kernels: 0 us -> 131 us
  matrix products: 24.7 us -> 0 us
  between operations: 13.8 us -> 0.64 us
  local copies, waits for them, and re-layouts: 0.01 us -> 7.64 us
  other arithmetic: 5.54 us -> 0 us
    reduce_scatter x1 -> x0, waiting for transfers between devices: 149 us -> none  [on_device(): lax.psum_scatter(lax.dot_general(picked, down_weight, (((1,), (1,)), ((),...]
    all_gather x2 -> x0, waiting for transfers between devices: 149 us -> none  [the longest x1 84.3 us: on_device(): lax.all_gather(hidden, 'row', axis=0, tiled=True)]
    pallas_call x0 -> x1, Pallas kernels: none -> 131 us  [on_device(): pl.pallas_call(kernel, out_shape=(jax.ShapeDtypeStruct((tok, ff), jnp.bfl...]
    dot_general x2 -> x0, matrix products: 24.7 us -> none  [the longest x1 12.4 us: on_device(): lax.dot_general(picked, down_weight, (((1,), (1,)), ((), ())), preferred_...]
    unnamed x2 -> x3, local copies, waits for them, and re-layouts: 0.01 us -> 7.64 us
  transfers between devices with their start and end apart: 3 -> 0, of which waited for: 3 -> 0; matrix products, arithmetic and copies ran while one was open for 0% -> 0% of each run, Pallas kernels for 0% -> 0%
where the time goes in v1:
time: 140 us
  Pallas kernels  131 us (94%)
  local copies, waits for them, and re-layouts  7.64 us (5%)
    pallas_call x1, Pallas kernels, on_device(): pl.pallas_call(kernel, out_shape=(jax.ShapeDtypeStruct((tok, ff), jnp.bfl...  131 us
    unnamed x3, local copies, waits for them, and re-layouts  7.64 us

profile of v1, /device:TPU:32, one launch (start us, length us, event | category | flops | bytes accessed | tf_op | source)
XLA Modules:
  0.0 139.6 jit_solution(8399862173614748402)
XLA Ops:
  0.6 131.4 %down_backward.1 = (bf16[128,1664]{1,0:T(8,128)(2,1)}, bf16[128,1664]{1,0:T(8,128)(2,1)}, bf16[1664,1024]{1,0:T(8,128)(2,1)}) custom-call(s32[16]{0:T(128)} %counts_ref.1, bf16[128,1024]{1,0:T(8,128)(2,1)} %cot_ref.1, bf16[128,1664]{1,0:T(8,128)(2,1)} %gate_ref.1, bf16[128,1664]{1,0:T(8,128)(2,1)} %up_ref.1, bf16[1664,1024]{1,0:T(8,128)(2,1)} %weight_hbm.1), custom_call_target="tpu_custom_call" | custom-call | flops 13958643712 | bytes 8519680 | tf_op jit(solution)/shard_map/down_backward/pallas_call | solution.py:278
  132.0 1.8 %copy.11 = bf16[128,1664]{1,0:T(8,128)(2,1)} copy(bf16[128,1664]{1,0:T(8,128)(2,1)} %get-tuple-element.6) | data formatting | bytes 851968
  133.8 1.8 %copy.12 = bf16[128,1664]{1,0:T(8,128)(2,1)} copy(bf16[128,1664]{1,0:T(8,128)(2,1)} %get-tuple-element.7) | data formatting | bytes 851968
  135.6 4.1 %copy.13 = bf16[1664,1024]{1,0:T(8,128)(2,1)} copy(bf16[1664,1024]{1,0:T(8,128)(2,1)} %get-tuple-element.8) | data formatting | bytes 6815744

commit v2 on v1

--- a/solution.py
+++ b/solution.py
@@ -1,3 +1,5 @@
+import functools
+
 import jax
 import jax.numpy as jnp
 from jax import lax
@@ -10,14 +12,26 @@
 TOK = 128
 LANES = 128
 HOPS = 8
-CYCLES = (
-    ("zig", 0, 0, 4),
-    ("zig", 1, 4, 4),
-    ("loop", 0, 8, 1),
-    ("loop", 1, 9, 1),
-    ("loop", 3, 10, 1),
-    ("loop", 4, 11, 1),
-    ("loop", 6, 12, 1),
+HALF = 64
+
+
+def streams(*rows):
+    first, out = 0, []
+    for kind, cut, longer, count in rows:
+        out.append((kind, cut, longer, first, count))
+        first += count
+    return tuple(out)
+
+
+GATHER = streams(
+    ("zig", 1, 0, 4), ("zig", 0, 0, 3), ("zig", 0, 1, 3), ("zig", 1, 1, 2),
+    ("loop", 1, 1, 2), ("loop", 2, 1, 2), ("loop", 3, 0, 2), ("loop", 4, 0, 2),
+    ("loop", 6, 0, 2), ("loop", 7, 1, 2), ("loop", 0, 0, 1), ("loop", 5, 1, 1),
+)
+SCATTER = streams(
+    ("zig", 0, 0, 4), ("zig", 1, 1, 4), ("zig", 0, 1, 3), ("zig", 1, 0, 3),
+    ("loop", 1, 0, 2), ("loop", 3, 0, 2), ("loop", 5, 1, 2), ("loop", 7, 0, 2),
+    ("loop", 0, 1, 1), ("loop", 2, 1, 1), ("loop", 4, 1, 1), ("loop", 6, 1, 1),
 )
 TILES = 13
 SOURCES = ((0, 0), (1, 0), (0, 1), (0, 3), (0, 2), (1, 1), (1, 3), (1, 2))
@@ -45,15 +59,15 @@
     return x * (15 - z) + (1 - x) * z
 
 
-def hops_of(i, d):
-    return HOPS if (i + d) % 2 == 0 else HOPS - 1
+def hops_of(cycle, d):
+    return HOPS if d == cycle[2] else HOPS - 1
 
 
 def kernel(
     counts_ref, cot_ref, gate_ref, up_ref, weight_hbm,
     grad_gate_ref, grad_up_ref, grad_down_ref,
-    weight, cot, hid, part, stage, arrived,
-    weight_sem, cot_send, cot_recv, core_send, core_recv,
+    weight, cot, hid, part, stage, arrived, factors, down_out,
+    weight_sem, down_sem, cot_send, cot_recv, core_send, core_recv,
     hid_send, hid_recv, sum_send, sum_recv,
 ):
     row = lax.axis_index("row")
@@ -127,12 +141,12 @@
         )
 
     def hid_copy(i, d, s, shift=0):
-        cycle = CYCLES[i]
+        cycle = GATHER[i]
         p = spot(cycle, row)
         way = 1 - 2 * d
         block = hid.at[
             place(cycle, p - way * (s + shift)),
-            pl.ds(cycle[2] * LANES, cycle[3] * LANES),
+            pl.ds(cycle[3] * HALF, cycle[4] * HALF),
         ]
         return pltpu.make_async_remote_copy(
             src_ref=block, dst_ref=block, send_sem=hid_send.at[i, d, s], recv_sem=hid_recv.at[i, d, s],
@@ -140,18 +154,18 @@
         )
 
     def sum_copy(i, d, s):
-        cycle = CYCLES[i]
-        tiles = pl.ds(cycle[2], cycle[3])
+        cycle = SCATTER[i]
+        tiles = pl.ds(cycle[3], cycle[4])
         return pltpu.make_async_remote_copy(
             src_ref=stage.at[d, s, tiles], dst_ref=arrived.at[d, s, tiles],
             send_sem=sum_send.at[i, d, s], recv_sem=sum_recv.at[i, d, s],
             device_id={"row": place(cycle, spot(cycle, row) + 1 - 2 * d)}, device_id_type=MESH,
         )
 
-    def each(s, run):
-        for i in range(len(CYCLES)):
+    def each(walks, s, run):
+        for i, cycle in enumerate(walks):
             for d in range(2):
-                if hops_of(i, d) < HOPS:
+                if hops_of(cycle, d) < HOPS:
                     pl.when(s < HOPS - 1)(lambda i=i, d=d: run(i, d))
                 else:
                     run(i, d)
@@ -170,7 +184,7 @@
 
                 hid_copy(i, d, s).start()
 
-            each(s, run)
+            each(GATHER, s, run)
 
         @pl.when((s > 0) & (s < HOPS))
         def _():
@@ -197,7 +211,7 @@
                 )
                 for k in range(n):
                     piece = product[:, k * LANES:(k + 1) * LANES]
-                    part[pl.ds(first, 2), t + k] = piece.reshape(2, TOK, LANES)
+                    part[pl.ds(first, 2), 2 * (t + k):2 * (t + k) + 2] = piece.reshape(2, 2, HALF, LANES)
 
         return carry
 
@@ -205,9 +219,9 @@
 
     def sum_send_step(s, received):
         def run(i, d):
-            cycle = CYCLES[i]
-            tiles = pl.ds(cycle[2], cycle[3])
-            owner = place(cycle, spot(cycle, row) + (1 - 2 * d) * (hops_of(i, d) - s))
+            cycle = SCATTER[i]
+            tiles = pl.ds(cycle[3], cycle[4])
+            owner = place(cycle, spot(cycle, row) + (1 - 2 * d) * (hops_of(cycle, d) - s))
             value = part[owner, tiles]
             if received:
                 sum_copy(i, d, s - 1).wait_recv()
@@ -215,16 +229,16 @@
             stage[d, s, tiles] = value.astype(jnp.bfloat16)
             sum_copy(i, d, s).start()
 
-        each(s, run)
+        each(SCATTER, s, run)
 
     sum_send_step(0, False)
-    for i in range(len(CYCLES)):
+    for i, cycle in enumerate(GATHER):
         for d in range(2):
-            hid_copy(i, d, hops_of(i, d) - 1, 1).wait_recv()
+            hid_copy(i, d, hops_of(cycle, d) - 1, 1).wait_recv()
 
     def down(first, n):
         lhs = jnp.concatenate([hid[g, pl.ds(first, n), :] for g in range(GROUPS)], axis=1)
-        grad_down_ref[pl.ds(first, n), :] = jnp.dot(
+        down_out[pl.ds(first, n), :] = jnp.dot(
             lhs, cot[...].reshape(GROUPS * TOK, cot.shape[2]), preferred_element_type=jnp.float32
         ).astype(jnp.bfloat16)
 
@@ -240,33 +254,77 @@
     lax.fori_loop(1, HOPS, sum_step, 0)
     down((TILES - 1) * LANES, LANES)
 
-    for i, (kind, cut, first, count) in enumerate(CYCLES):
+    store_down = pltpu.make_async_copy(down_out, grad_down_ref, down_sem)
+    store_down.start()
+
+    for t in range(TILES):
+        lanes = pl.ds(t * LANES, LANES)
+        g = gate_ref[:, lanes].astype(jnp.float32)
+        u = up_ref[:, lanes].astype(jnp.float32)
+        sig = jax.nn.sigmoid(g)
+        factors[0, t] = g * sig
+        factors[1, t] = u * (sig * (1.0 + g * (1.0 - sig)))
+
+    for i, cycle in enumerate(SCATTER):
+        tiles = pl.ds(cycle[3], cycle[4])
+        total = part[row, tiles]
         for d in range(2):
-            sum_copy(i, d, hops_of(i, d) - 1).wait_recv()
-        for t in range(first, first + count):
-            lanes = pl.ds(t * LANES, LANES)
-            grad = part[row, t]
-            for d in range(2):
-                grad = grad + arrived[d, hops_of(i, d) - 1, t].astype(jnp.float32)
-            g = gate_ref[:, lanes].astype(jnp.float32)
-            u = up_ref[:, lanes].astype(jnp.float32)
-            sig = jax.nn.sigmoid(g)
-            grad_up_ref[:, lanes] = (grad * (g * sig)).astype(jnp.bfloat16)
-            slope = sig * (1.0 + g * (1.0 - sig))
-            grad_gate_ref[:, lanes] = (grad * u * slope).astype(jnp.bfloat16)
+            sum_copy(i, d, hops_of(cycle, d) - 1).wait_recv()
+            total = total + arrived[d, hops_of(cycle, d) - 1, tiles].astype(jnp.float32)
+        part[row, tiles] = total
+    for t in range(TILES):
+        lanes = pl.ds(t * LANES, LANES)
+        grad = part[row, 2 * t:2 * t + 2].reshape(TOK, LANES)
+        grad_up_ref[:, lanes] = (grad * factors[0, t]).astype(jnp.bfloat16)
+        grad_gate_ref[:, lanes] = (grad * factors[1, t]).astype(jnp.bfloat16)
 
     def drain(s, carry):
-        def run(i, d):
-            hid_copy(i, d, s).wait_send()
-            sum_copy(i, d, s).wait_send()
-
-        each(s, run)
+        each(GATHER, s, lambda i, d: hid_copy(i, d, s).wait_send())
+        each(SCATTER, s, lambda i, d: sum_copy(i, d, s).wait_send())
         core_copy(s).wait_send()
         return carry
 
     lax.fori_loop(0, HOPS, drain, 0)
     for q in range(1, 8):
         cot_copy(q).wait_send()
+    store_down.wait()
+
+
+def copy_kernel(pieces, *refs):
+    n = len(refs) // 3
+    take, give = refs[-2], refs[-1]
+    steps, k = [], 0
+    for a in range(n):
+        source, target, held = refs[a], refs[n + a], refs[2 * n + a]
+        rows = source.shape[0] // pieces[a]
+        for p in range(pieces[a]):
+            part = pl.ds(p * rows, rows)
+            steps.append((
+                pltpu.make_async_copy(source.at[part], held.at[part], take.at[k]),
+                pltpu.make_async_copy(held.at[part], target.at[part], give.at[k]),
+            ))
+            k += 1
+    for step in steps:
+        step[0].start()
+    for step in steps:
+        step[0].wait()
+        step[1].start()
+    for step in steps:
+        step[1].wait()
+
+
+def copied(pieces, *arrays):
+    anywhere = pl.BlockSpec(memory_space=pl.ANY)
+    sems = pltpu.SemaphoreType.DMA((sum(pieces),))
+    return pl.pallas_call(
+        functools.partial(copy_kernel, pieces),
+        out_shape=tuple(jax.ShapeDtypeStruct(a.shape, a.dtype) for a in arrays),
+        in_specs=[anywhere] * len(arrays),
+        out_specs=(anywhere,) * len(arrays),
+        scratch_shapes=[pltpu.VMEM(a.shape, a.dtype) for a in arrays] + [sems, sems],
+        compiler_params=pltpu.CompilerParams(vmem_limit_bytes=16 * 2**20),
+        name="copy_out",
+    )(*arrays)
 
 
 def on_device(counts, cotangent, saved_gate, saved_up, down_weight):
@@ -274,8 +332,7 @@
     d = cotangent.shape[1]
     vmem = pl.BlockSpec(memory_space=pltpu.VMEM)
     dma = pltpu.SemaphoreType.DMA
-    n = len(CYCLES)
-    return pl.pallas_call(
+    results = pl.pallas_call(
         kernel,
         out_shape=(
             jax.ShapeDtypeStruct((tok, ff), jnp.bfloat16),
@@ -285,16 +342,19 @@
         in_specs=[
             pl.BlockSpec(memory_space=pltpu.SMEM), vmem, vmem, vmem, pl.BlockSpec(memory_space=pl.ANY),
         ],
-        out_specs=(vmem, vmem, vmem),
+        out_specs=(vmem, vmem, pl.BlockSpec(memory_space=pl.ANY)),
         scratch_shapes=[
             pltpu.VMEM((ff, d), jnp.bfloat16),
             pltpu.VMEM((GROUPS, tok, d), jnp.bfloat16),
             pltpu.VMEM((GROUPS, ff, tok), jnp.bfloat16),
-            pltpu.VMEM((GROUPS, TILES, tok, LANES), jnp.float32),
-            pltpu.VMEM((2, HOPS, TILES, tok, LANES), jnp.bfloat16),
-            pltpu.VMEM((2, HOPS, TILES, tok, LANES), jnp.bfloat16),
-            dma, dma((8,)), dma((8,)), dma((8,)), dma((8,)),
-            dma((n, 2, HOPS)), dma((n, 2, HOPS)), dma((n, 2, HOPS)), dma((n, 2, HOPS)),
+            pltpu.VMEM((GROUPS, 2 * TILES, HALF, LANES), jnp.float32),
+            pltpu.VMEM((2, HOPS, 2 * TILES, HALF, LANES), jnp.bfloat16),
+            pltpu.VMEM((2, HOPS, 2 * TILES, HALF, LANES), jnp.bfloat16),
+            pltpu.VMEM((2, TILES, tok, LANES), jnp.float32),
+            pltpu.VMEM((ff, d), jnp.bfloat16),
+            dma, dma, dma((8,)), dma((8,)), dma((8,)), dma((8,)),
+            dma((len(GATHER), 2, HOPS)), dma((len(GATHER), 2, HOPS)),
+            dma((len(SCATTER), 2, HOPS)), dma((len(SCATTER), 2, HOPS)),
         ],
         compiler_params=pltpu.CompilerParams(
             collective_id=0, has_side_effects=True, vmem_limit_bytes=60 * 2**20
@@ -304,6 +364,7 @@
         ),
         name="down_backward",
     )(counts, cotangent, saved_gate, saved_up, down_weight)
+    return copied((1, 1, 4), *results)
 
 
 def solution(mesh):

time: 140 us -> 131 us (0.936); the launches traced: 140 us -> 129 us
  Pallas kernels: 131 us -> 124 us
  local copies, waits for them, and re-layouts: 7.64 us -> 3.97 us
    pallas_call x1, Pallas kernels: 131 us -> 121 us  [on_device(): pl.pallas_call(kernel, out_shape=(jax.ShapeDtypeStruct((tok, ff), jnp.bfl...]
    unnamed x3 -> x6, local copies, waits for them, and re-layouts: 7.64 us -> 3.97 us
    pallas_call x0 -> x1, Pallas kernels: none -> 3.13 us  [copied(): pl.pallas_call(functools.partial(copy_kernel, pieces), out_shape=tuple((j...]
where the time goes in v2:
time: 131 us; the launch traced here: 129 us
  Pallas kernels  124 us (95%)
  local copies, waits for them, and re-layouts  3.97 us (3%)
    pallas_call x1, Pallas kernels, on_device(): pl.pallas_call(kernel, out_shape=(jax.ShapeDtypeStruct((tok, ff), jnp.bfl...  121 us
    unnamed x6, local copies, waits for them, and re-layouts  3.97 us
    pallas_call x1, Pallas kernels, copied(): pl.pallas_call(functools.partial(copy_kernel, pieces), out_shape=tuple((j...  3.13 us

profile of v2, /device:TPU:32, one launch (start us, length us, event | category | flops | bytes accessed | tf_op | source)
XLA Modules:
  0.0 128.6 jit_solution(14829076480438662230)
XLA Ops:
  0.6 120.9 %down_backward.1 = (bf16[128,1664]{1,0:T(8,128)(2,1)}, bf16[128,1664]{1,0:T(8,128)(2,1)}, bf16[1664,1024]{1,0:T(8,128)(2,1)}) custom-call(s32[16]{0:T(128)} %counts_ref.1, bf16[128,1024]{1,0:T(8,128)(2,1)} %cot_ref.1, bf16[128,1664]{1,0:T(8,128)(2,1)} %gate_ref.1, bf16[128,1664]{1,0:T(8,128)(2,1)} %up_ref.1, bf16[1664,1024]{1,0:T(8,128)(2,1)} %weight_hbm.1), custom_call_target="tpu_custom_call" | custom-call | flops 13958643712 | bytes 8519680 | tf_op jit(solution)/shard_map/down_backward/pallas_call | solution.py:335
  121.5 0.0 copy-start
  121.5 2.0 %copy-done = bf16[1664,1024]{1,0:T(8,128)(2,1)S(1)} copy-done((bf16[1664,1024]{1,0:T(8,128)(2,1)S(1)}, bf16[1664,1024]{1,0:T(8,128)(2,1)}, u32[]{:S(2)}) %copy-start) | copy-done | bytes 3407896
  123.5 0.0 copy-start.1
  123.5 1.0 copy-done.1
  124.5 0.0 copy-start.2
  124.5 1.0 copy-done.2
  125.5 3.1 %copy_out.1 = (bf16[128,1664]{1,0:T(8,128)(2,1)}, bf16[128,1664]{1,0:T(8,128)(2,1)}, bf16[1664,1024]{1,0:T(8,128)(2,1)}) custom-call(bf16[128,1664]{1,0:T(8,128)(2,1)S(1)} %copy-done.1, bf16[128,1664]{1,0:T(8,128)(2,1)S(1)} %copy-done.2, bf16[1664,1024]{1,0:T(8,128)(2,1)S(1)} %copy-done), custom_call_target="tpu_custom_call" | custom-call | tf_op jit(solution)/shard_map/copy_out/pallas_call | solution.py:319
Async XLA Ops:
  121.5 2.0 %copy-start = (bf16[1664,1024]{1,0:T(8,128)(2,1)S(1)}, bf16[1664,1024]{1,0:T(8,128)(2,1)}, u32[]{:S(2)}) copy-start(bf16[1664,1024]{1,0:T(8,128)(2,1)} %get-tuple-element.8.refs_2_) | copy-start | bytes 10223620
  123.5 1.0 copy-start.1
  124.5 1.0 copy-start.2

commit v3 on v2

--- a/solution.py
+++ b/solution.py
@@ -24,15 +24,14 @@
 
 
 GATHER = streams(
-    ("zig", 1, 0, 4), ("zig", 0, 0, 3), ("zig", 0, 1, 3), ("zig", 1, 1, 2),
-    ("loop", 1, 1, 2), ("loop", 2, 1, 2), ("loop", 3, 0, 2), ("loop", 4, 0, 2),
-    ("loop", 6, 0, 2), ("loop", 7, 1, 2), ("loop", 0, 0, 1), ("loop", 5, 1, 1),
+    ("zig", 1, 0, 4), ("zig", 0, 1, 3), ("loop", 1, 1, 2), ("loop", 3, 0, 2), ("loop", 6, 0, 2), ("loop", 0, 0, 1),
+    ("zig", 0, 0, 3), ("zig", 1, 1, 2), ("loop", 2, 1, 2), ("loop", 4, 0, 2), ("loop", 7, 1, 2), ("loop", 5, 1, 1),
 )
 SCATTER = streams(
-    ("zig", 0, 0, 4), ("zig", 1, 1, 4), ("zig", 0, 1, 3), ("zig", 1, 0, 3),
-    ("loop", 1, 0, 2), ("loop", 3, 0, 2), ("loop", 5, 1, 2), ("loop", 7, 0, 2),
-    ("loop", 0, 1, 1), ("loop", 2, 1, 1), ("loop", 4, 1, 1), ("loop", 6, 1, 1),
+    ("zig", 0, 0, 4), ("zig", 1, 1, 4), ("loop", 1, 0, 2), ("loop", 5, 1, 2), ("loop", 0, 1, 1), ("loop", 4, 1, 1),
+    ("zig", 0, 1, 3), ("zig", 1, 0, 3), ("loop", 3, 0, 2), ("loop", 7, 0, 2), ("loop", 2, 1, 1), ("loop", 6, 1, 1),
 )
+SETS = (range(0, 6), range(6, 12))
 TILES = 13
 SOURCES = ((0, 0), (1, 0), (0, 1), (0, 3), (0, 2), (1, 1), (1, 3), (1, 2))
 
@@ -64,10 +63,10 @@
 
 
 def kernel(
-    counts_ref, cot_ref, gate_ref, up_ref, weight_hbm,
+    counts_ref, cot_hbm, gate_hbm, up_hbm, weight_hbm,
     grad_gate_ref, grad_up_ref, grad_down_ref,
-    weight, cot, hid, part, stage, arrived, factors, down_out,
-    weight_sem, down_sem, cot_send, cot_recv, core_send, core_recv,
+    cot_ref, gate_ref, up_ref, weight, cot, hid, part, stage, arrived, factors, down_out,
+    load_sem, down_sem, cot_send, cot_recv, core_send, core_recv,
     hid_send, hid_recv, sum_send, sum_recv,
 ):
     row = lax.axis_index("row")
@@ -80,8 +79,10 @@
     def at_col(dx, dy, c):
         return lax.rem(xh + dx, 2) * 8 + lax.rem(y + dy, 4) * 2 + c
 
-    load_weight = pltpu.make_async_copy(weight_hbm, weight, weight_sem)
-    load_weight.start()
+    pairs = ((cot_hbm, cot_ref), (gate_hbm, gate_ref), (up_hbm, up_ref), (weight_hbm, weight))
+    loads = [pltpu.make_async_copy(*pair, load_sem.at[k]) for k, pair in enumerate(pairs)]
+    for load in loads:
+        load.start()
 
     barrier = pltpu.get_barrier_semaphore()
     rows = [(1 - x) * 8 + z, x * 8 + lax.rem(z + 1, 8), x * 8 + lax.rem(z + 7, 8)]
@@ -93,12 +94,8 @@
 
     limit = counts_ref[col]
     token = lax.broadcasted_iota(jnp.int32, cot_ref.shape, 0)
+    loads[0].wait()
     cot[col] = jnp.where(token < limit, cot_ref[...], jnp.zeros_like(cot_ref))
-    for t in range(TILES):
-        lanes = pl.ds(t * LANES, LANES)
-        g = gate_ref[:, lanes].astype(jnp.float32)
-        u = up_ref[:, lanes].astype(jnp.float32)
-        hid[row, lanes, :] = (g * jax.nn.sigmoid(g) * u).T.astype(jnp.bfloat16)
     pl.semaphore_wait(barrier, len(rows) + len(cols))
 
     def cot_copy(q):
@@ -162,8 +159,9 @@
             device_id={"row": place(cycle, spot(cycle, row) + 1 - 2 * d)}, device_id_type=MESH,
         )
 
-    def each(walks, s, run):
-        for i, cycle in enumerate(walks):
+    def each(walks, s, run, picks=range(12)):
+        for i in picks:
+            cycle = walks[i]
             for d in range(2):
                 if hops_of(cycle, d) < HOPS:
                     pl.when(s < HOPS - 1)(lambda i=i, d=d: run(i, d))
@@ -174,50 +172,70 @@
         cot_copy(q).start()
     core_copy(0).start()
 
+    loads[1].wait()
+    loads[2].wait()
+    tiles_done = 0
+    for i, cycle in enumerate(GATHER):
+        while 2 * tiles_done < cycle[3] + cycle[4]:
+            lanes = pl.ds(tiles_done * LANES, LANES)
+            g = gate_ref[:, lanes].astype(jnp.float32)
+            u = up_ref[:, lanes].astype(jnp.float32)
+            hid[row, lanes, :] = (g * jax.nn.sigmoid(g) * u).T.astype(jnp.bfloat16)
+            tiles_done += 1
+        for d in range(2):
+            hid_copy(i, d, 0).start()
+    loads[3].wait()
+
+    def pass_on(s, picks):
+        def run(i, d):
+            hid_copy(i, d, s - 1, 1).wait_recv()
+            hid_copy(i, d, s).start()
+
+        each(GATHER, s, run, picks)
+
+    def partial_sums(q, carry):
+        core_arrival(q).wait_recv()
+        dx, dy = source(q)
+        first = at_col(dx, dy, 0)
+        block = cot[pl.ds(first, 2)].reshape(2 * TOK, cot.shape[2])
+        for t in range(0, TILES, 2):
+            n = min(2, TILES - t)
+            product = lax.dot_general(
+                block, weight[t * LANES:(t + n) * LANES, :], (((1,), (1,)), ((), ())),
+                preferred_element_type=jnp.float32,
+            )
+            for k in range(n):
+                piece = product[:, k * LANES:(k + 1) * LANES]
+                part[pl.ds(first, 2), 2 * (t + k):2 * (t + k) + 2] = piece.reshape(2, 2, HALF, LANES)
+        return carry
+
+    def across(q, carry):
+        cot_arrival(q).wait_recv()
+        core_copy(q).start()
+        return carry
+
+    def after(s):
+        return lax.div(3 * s + 2, 2)
+
     def gather_step(s, carry):
-        @pl.when(s < HOPS)
+        pass_on(s, SETS[0])
+
+        @pl.when(s < 6)
         def _():
-            def run(i, d):
-                @pl.when(s > 0)
-                def _():
-                    hid_copy(i, d, s - 1, 1).wait_recv()
-
-                hid_copy(i, d, s).start()
-
-            each(GATHER, s, run)
-
-        @pl.when((s > 0) & (s < HOPS))
-        def _():
-            cot_arrival(s).wait_recv()
-            core_copy(s).start()
+            lax.fori_loop(after(s - 1), after(s), across, 0)
 
         @pl.when(s == 1)
         def _():
             for q in range(5, 8):
                 cot_copy(q).start()
-            load_weight.wait()
-
-        @pl.when(s > 0)
-        def _():
-            core_arrival(s - 1).wait_recv()
-            dx, dy = source(s - 1)
-            first = at_col(dx, dy, 0)
-            block = cot[pl.ds(first, 2)].reshape(2 * TOK, cot.shape[2])
-            for t in range(0, TILES, 2):
-                n = min(2, TILES - t)
-                product = lax.dot_general(
-                    block, weight[t * LANES:(t + n) * LANES, :], (((1,), (1,)), ((), ())),
-                    preferred_element_type=jnp.float32,
-                )
-                for k in range(n):
-                    piece = product[:, k * LANES:(k + 1) * LANES]
-                    part[pl.ds(first, 2), 2 * (t + k):2 * (t + k) + 2] = piece.reshape(2, 2, HALF, LANES)
-
-        return carry
-
-    lax.fori_loop(0, HOPS + 1, gather_step, 0)
-
-    def sum_send_step(s, received):
+
+        lax.fori_loop(jnp.where(s == 1, 0, after(s - 2)), after(s - 1), partial_sums, 0)
+        pass_on(s, SETS[1])
+        return carry
+
+    lax.fori_loop(1, HOPS - 1, gather_step, 0)
+
+    def sum_send_step(s, received, picks):
         def run(i, d):
             cycle = SCATTER[i]
             tiles = pl.ds(cycle[3], cycle[4])
@@ -229,12 +247,11 @@
             stage[d, s, tiles] = value.astype(jnp.bfloat16)
             sum_copy(i, d, s).start()
 
-        each(SCATTER, s, run)
-
-    sum_send_step(0, False)
-    for i, cycle in enumerate(GATHER):
-        for d in range(2):
-            hid_copy(i, d, hops_of(cycle, d) - 1, 1).wait_recv()
+        each(SCATTER, s, run, picks)
+
+    for picks in SETS:
+        sum_send_step(0, False, picks)
+        pass_on(HOPS - 1, picks)
 
     def down(first, n):
         lhs = jnp.concatenate([hid[g, pl.ds(first, n), :] for g in range(GROUPS)], axis=1)
@@ -242,13 +259,24 @@
             lhs, cot[...].reshape(GROUPS * TOK, cot.shape[2]), preferred_element_type=jnp.float32
         ).astype(jnp.bfloat16)
 
+    def down_piece(k, carry):
+        down(pl.multiple_of(k * 2 * LANES, 2 * LANES), 2 * LANES)
+        return carry
+
     def sum_step(s, carry):
-        sum_send_step(s, True)
-
-        @pl.when(s < HOPS - 1)
+        sum_send_step(s, True, SETS[0])
+
+        @pl.when(s == 1)
         def _():
-            down(pl.multiple_of((s - 1) * 2 * LANES, 2 * LANES), 2 * LANES)
-
+            for i, cycle in enumerate(GATHER):
+                for d in range(2):
+                    hid_copy(i, d, hops_of(cycle, d) - 1, 1).wait_recv()
+
+        @pl.when(s > 1)
+        def _():
+            down_piece(s - 2, 0)
+
+        sum_send_step(s, True, SETS[1])
         return carry
 
     lax.fori_loop(1, HOPS, sum_step, 0)
@@ -322,7 +350,7 @@
         in_specs=[anywhere] * len(arrays),
         out_specs=(anywhere,) * len(arrays),
         scratch_shapes=[pltpu.VMEM(a.shape, a.dtype) for a in arrays] + [sems, sems],
-        compiler_params=pltpu.CompilerParams(vmem_limit_bytes=16 * 2**20),
+        compiler_params=pltpu.CompilerParams(vmem_limit_bytes=60 * 2**20),
         name="copy_out",
     )(*arrays)
 
@@ -331,6 +359,7 @@
     tok, ff = saved_gate.shape
     d = cotangent.shape[1]
     vmem = pl.BlockSpec(memory_space=pltpu.VMEM)
+    anywhere = pl.BlockSpec(memory_space=pl.ANY)
     dma = pltpu.SemaphoreType.DMA
     results = pl.pallas_call(
         kernel,
@@ -340,10 +369,13 @@
             jax.ShapeDtypeStruct((ff, d), jnp.bfloat16),
         ),
         in_specs=[
-            pl.BlockSpec(memory_space=pltpu.SMEM), vmem, vmem, vmem, pl.BlockSpec(memory_space=pl.ANY),
+            pl.BlockSpec(memory_space=pltpu.SMEM), anywhere, anywhere, anywhere, anywhere,
         ],
-        out_specs=(vmem, vmem, pl.BlockSpec(memory_space=pl.ANY)),
+        out_specs=(vmem, vmem, anywhere),
         scratch_shapes=[
+            pltpu.VMEM((tok, d), jnp.bfloat16),
+            pltpu.VMEM((tok, ff), jnp.bfloat16),
+            pltpu.VMEM((tok, ff), jnp.bfloat16),
             pltpu.VMEM((ff, d), jnp.bfloat16),
             pltpu.VMEM((GROUPS, tok, d), jnp.bfloat16),
             pltpu.VMEM((GROUPS, ff, tok), jnp.bfloat16),
@@ -352,7 +384,7 @@
             pltpu.VMEM((2, HOPS, 2 * TILES, HALF, LANES), jnp.bfloat16),
             pltpu.VMEM((2, TILES, tok, LANES), jnp.float32),
             pltpu.VMEM((ff, d), jnp.bfloat16),
-            dma, dma, dma((8,)), dma((8,)), dma((8,)), dma((8,)),
+            dma((4,)), dma, dma((8,)), dma((8,)), dma((8,)), dma((8,)),
             dma((len(GATHER), 2, HOPS)), dma((len(GATHER), 2, HOPS)),
             dma((len(SCATTER), 2, HOPS)), dma((len(SCATTER), 2, HOPS)),
         ],

time: 131 us -> 123 us (0.939)
  Pallas kernels: 124 us -> 120 us
  local copies, waits for them, and re-layouts: 3.97 us -> 0 us
    pallas_call x1, Pallas kernels: 121 us -> 117 us  [on_device(): pl.pallas_call(kernel, out_shape=(jax.ShapeDtypeStruct((tok, ff), jnp.bfl...]
    unnamed x6 -> x0, local copies, waits for them, and re-layouts: 3.97 us -> none
where the time goes in v3:
time: 123 us; the launch traced here: 121 us
  Pallas kernels  120 us (98%)
    pallas_call x1, Pallas kernels, on_device(): pl.pallas_call(kernel, out_shape=(jax.ShapeDtypeStruct((tok, ff), jnp.bfl...  117 us
    pallas_call x1, Pallas kernels, copied(): pl.pallas_call(functools.partial(copy_kernel, pieces), out_shape=tuple((j...  3.86 us

profile of v3, /device:TPU:32, one launch (start us, length us, event | category | flops | bytes accessed | tf_op | source)
XLA Modules:
  0.0 121.0 jit_solution(12008309312195450495)
XLA Ops:
  0.6 116.5 %down_backward.1 = (bf16[128,1664]{1,0:T(8,128)(2,1)}, bf16[128,1664]{1,0:T(8,128)(2,1)}, bf16[1664,1024]{1,0:T(8,128)(2,1)}) custom-call(s32[16]{0:T(128)} %counts_ref.1, bf16[128,1024]{1,0:T(8,128)(2,1)} %cot_hbm.1, bf16[128,1664]{1,0:T(8,128)(2,1)} %gate_hbm.1, bf16[128,1664]{1,0:T(8,128)(2,1)} %up_hbm.1, bf16[1664,1024]{1,0:T(8,128)(2,1)} %weight_hbm.1), custom_call_target="tpu_custom_call" | custom-call | flops 13958643712 | bytes 8519680 | tf_op jit(solution)/shard_map/down_backward/pallas_call | solution.py:364
  117.1 3.9 %copy_out.1 = (bf16[128,1664]{1,0:T(8,128)(2,1)}, bf16[128,1664]{1,0:T(8,128)(2,1)}, bf16[1664,1024]{1,0:T(8,128)(2,1)}) custom-call(bf16[128,1664]{1,0:T(8,128)(2,1)} %get-tuple-element.6.refs_0_, bf16[128,1664]{1,0:T(8,128)(2,1)} %get-tuple-element.7.refs_1_, bf16[1664,1024]{1,0:T(8,128)(2,1)} %get-tuple-element.8.refs_2_), custom_call_target="tpu_custom_call" | custom-call | tf_op jit(solution)/shard_map/copy_out/pallas_call | solution.py:347

commit v4 on v3

--- a/solution.py
+++ b/solution.py
@@ -146,7 +146,7 @@
             pl.ds(cycle[3] * HALF, cycle[4] * HALF),
         ]
         return pltpu.make_async_remote_copy(
-            src_ref=block, dst_ref=block, send_sem=hid_send.at[i, d, s], recv_sem=hid_recv.at[i, d, s],
+            src_ref=block, dst_ref=block, send_sem=hid_send, recv_sem=hid_recv.at[i, d, s],
             device_id={"row": place(cycle, p + way)}, device_id_type=MESH,
         )
 
@@ -155,7 +155,7 @@
         tiles = pl.ds(cycle[3], cycle[4])
         return pltpu.make_async_remote_copy(
             src_ref=stage.at[d, s, tiles], dst_ref=arrived.at[d, s, tiles],
-            send_sem=sum_send.at[i, d, s], recv_sem=sum_recv.at[i, d, s],
+            send_sem=sum_send, recv_sem=sum_recv.at[i, d, s],
             device_id={"row": place(cycle, spot(cycle, row) + 1 - 2 * d)}, device_id_type=MESH,
         )
 
@@ -306,13 +306,11 @@
         grad_up_ref[:, lanes] = (grad * factors[0, t]).astype(jnp.bfloat16)
         grad_gate_ref[:, lanes] = (grad * factors[1, t]).astype(jnp.bfloat16)
 
-    def drain(s, carry):
-        each(GATHER, s, lambda i, d: hid_copy(i, d, s).wait_send())
-        each(SCATTER, s, lambda i, d: sum_copy(i, d, s).wait_send())
-        core_copy(s).wait_send()
-        return carry
-
-    lax.fori_loop(0, HOPS, drain, 0)
+    blocks = hid.at[pl.ds(0, GROUPS - 1)]
+    for sem in (hid_send, sum_send):
+        pltpu.make_async_copy(blocks, blocks, sem).wait()
+    for q in range(8):
+        core_copy(q).wait_send()
     for q in range(1, 8):
         cot_copy(q).wait_send()
     store_down.wait()
@@ -385,8 +383,7 @@
             pltpu.VMEM((2, TILES, tok, LANES), jnp.float32),
             pltpu.VMEM((ff, d), jnp.bfloat16),
             dma((4,)), dma, dma((8,)), dma((8,)), dma((8,)), dma((8,)),
-            dma((len(GATHER), 2, HOPS)), dma((len(GATHER), 2, HOPS)),
-            dma((len(SCATTER), 2, HOPS)), dma((len(SCATTER), 2, HOPS)),
+            dma, dma((len(GATHER), 2, HOPS)), dma, dma((len(SCATTER), 2, HOPS)),
         ],
         compiler_params=pltpu.CompilerParams(
             collective_id=0, has_side_effects=True, vmem_limit_bytes=60 * 2**20
@@ -396,7 +393,7 @@
         ),
         name="down_backward",
     )(counts, cotangent, saved_gate, saved_up, down_weight)
-    return copied((1, 1, 4), *results)
+    return copied((1, 1, 2), *results)
 
 
 def solution(mesh):

time: 123 us -> 119 us (0.967)
  Pallas kernels: 120 us -> 117 us
    pallas_call x1, Pallas kernels: 117 us -> 113 us  [on_device(): pl.pallas_call(kernel, out_shape=(jax.ShapeDtypeStruct((tok, ff), jnp.bfl...]
where the time goes in v4:
time: 119 us; the launch traced here: 117 us
  Pallas kernels  117 us (98%)
    pallas_call x1, Pallas kernels, on_device(): pl.pallas_call(kernel, out_shape=(jax.ShapeDtypeStruct((tok, ff), jnp.bfl...  113 us
    pallas_call x1, Pallas kernels, copied(): pl.pallas_call(functools.partial(copy_kernel, pieces), out_shape=tuple((j...  3.8 us

profile of v4, /device:TPU:32, one launch (start us, length us, event | category | flops | bytes accessed | tf_op | source)
XLA Modules:
  0.0 117.2 jit_solution(3612130989351660095)
XLA Ops:
  0.6 112.7 %down_backward.1 = (bf16[128,1664]{1,0:T(8,128)(2,1)}, bf16[128,1664]{1,0:T(8,128)(2,1)}, bf16[1664,1024]{1,0:T(8,128)(2,1)}) custom-call(s32[16]{0:T(128)} %counts_ref.1, bf16[128,1024]{1,0:T(8,128)(2,1)} %cot_hbm.1, bf16[128,1664]{1,0:T(8,128)(2,1)} %gate_hbm.1, bf16[128,1664]{1,0:T(8,128)(2,1)} %up_hbm.1, bf16[1664,1024]{1,0:T(8,128)(2,1)} %weight_hbm.1), custom_call_target="tpu_custom_call" | custom-call | flops 13958643712 | bytes 8519680 | tf_op jit(solution)/shard_map/down_backward/pallas_call | solution.py:362
  113.4 3.8 %copy_out.1 = (bf16[128,1664]{1,0:T(8,128)(2,1)}, bf16[128,1664]{1,0:T(8,128)(2,1)}, bf16[1664,1024]{1,0:T(8,128)(2,1)}) custom-call(bf16[128,1664]{1,0:T(8,128)(2,1)} %get-tuple-element.6.refs_0_, bf16[128,1664]{1,0:T(8,128)(2,1)} %get-tuple-element.7.refs_1_, bf16[1664,1024]{1,0:T(8,128)(2,1)} %get-tuple-element.8.refs_2_), custom_call_target="tpu_custom_call" | custom-call | tf_op jit(solution)/shard_map/copy_out/pallas_call | solution.py:345

commit v5 on v4

--- a/solution.py
+++ b/solution.py
@@ -12,7 +12,8 @@
 TOK = 128
 LANES = 128
 HOPS = 8
-HALF = 64
+CUT = 32
+CUTS = TOK // CUT
 
 
 def streams(*rows):
@@ -24,12 +25,12 @@
 
 
 GATHER = streams(
-    ("zig", 1, 0, 4), ("zig", 0, 1, 3), ("loop", 1, 1, 2), ("loop", 3, 0, 2), ("loop", 6, 0, 2), ("loop", 0, 0, 1),
-    ("zig", 0, 0, 3), ("zig", 1, 1, 2), ("loop", 2, 1, 2), ("loop", 4, 0, 2), ("loop", 7, 1, 2), ("loop", 5, 1, 1),
+    ("zig", 0, 0, 6), ("zig", 1, 1, 6), ("loop", 0, 0, 3), ("loop", 2, 0, 3), ("loop", 4, 0, 3), ("loop", 6, 0, 3),
+    ("zig", 0, 1, 8), ("zig", 1, 0, 8), ("loop", 1, 1, 3), ("loop", 3, 1, 3), ("loop", 5, 1, 3), ("loop", 7, 1, 3),
 )
 SCATTER = streams(
-    ("zig", 0, 0, 4), ("zig", 1, 1, 4), ("loop", 1, 0, 2), ("loop", 5, 1, 2), ("loop", 0, 1, 1), ("loop", 4, 1, 1),
-    ("zig", 0, 1, 3), ("zig", 1, 0, 3), ("loop", 3, 0, 2), ("loop", 7, 0, 2), ("loop", 2, 1, 1), ("loop", 6, 1, 1),
+    ("zig", 0, 0, 6), ("zig", 1, 1, 6), ("loop", 0, 0, 3), ("loop", 2, 0, 3), ("loop", 4, 0, 3), ("loop", 6, 0, 3),
+    ("zig", 0, 1, 8), ("zig", 1, 0, 8), ("loop", 1, 1, 3), ("loop", 3, 1, 3), ("loop", 5, 1, 3), ("loop", 7, 1, 3),
 )
 SETS = (range(0, 6), range(6, 12))
 TILES = 13
@@ -143,7 +144,7 @@
         way = 1 - 2 * d
         block = hid.at[
             place(cycle, p - way * (s + shift)),
-            pl.ds(cycle[3] * HALF, cycle[4] * HALF),
+            pl.ds(cycle[3] * CUT, cycle[4] * CUT),
         ]
         return pltpu.make_async_remote_copy(
             src_ref=block, dst_ref=block, send_sem=hid_send, recv_sem=hid_recv.at[i, d, s],
@@ -176,7 +177,7 @@
     loads[2].wait()
     tiles_done = 0
     for i, cycle in enumerate(GATHER):
-        while 2 * tiles_done < cycle[3] + cycle[4]:
+        while CUTS * tiles_done < cycle[3] + cycle[4]:
             lanes = pl.ds(tiles_done * LANES, LANES)
             g = gate_ref[:, lanes].astype(jnp.float32)
             u = up_ref[:, lanes].astype(jnp.float32)
@@ -206,7 +207,7 @@
             )
             for k in range(n):
                 piece = product[:, k * LANES:(k + 1) * LANES]
-                part[pl.ds(first, 2), 2 * (t + k):2 * (t + k) + 2] = piece.reshape(2, 2, HALF, LANES)
+                part[pl.ds(first, 2), CUTS * (t + k):CUTS * (t + k + 1)] = piece.reshape(2, CUTS, CUT, LANES)
         return carry
 
     def across(q, carry):
@@ -302,9 +303,15 @@
         part[row, tiles] = total
     for t in range(TILES):
         lanes = pl.ds(t * LANES, LANES)
-        grad = part[row, 2 * t:2 * t + 2].reshape(TOK, LANES)
-        grad_up_ref[:, lanes] = (grad * factors[0, t]).astype(jnp.bfloat16)
-        grad_gate_ref[:, lanes] = (grad * factors[1, t]).astype(jnp.bfloat16)
+        grad = part[row, CUTS * t:CUTS * (t + 1)].reshape(TOK, LANES)
+        up_ref[:, lanes] = (grad * factors[0, t]).astype(jnp.bfloat16)
+        gate_ref[:, lanes] = (grad * factors[1, t]).astype(jnp.bfloat16)
+    stores = [
+        pltpu.make_async_copy(gate_ref, grad_gate_ref, load_sem.at[0]),
+        pltpu.make_async_copy(up_ref, grad_up_ref, load_sem.at[1]),
+    ]
+    for store in stores:
+        store.start()
 
     blocks = hid.at[pl.ds(0, GROUPS - 1)]
     for sem in (hid_send, sum_send):
@@ -314,6 +321,8 @@
     for q in range(1, 8):
         cot_copy(q).wait_send()
     store_down.wait()
+    for store in stores:
+        store.wait()
 
 
 def copy_kernel(pieces, *refs):
@@ -356,7 +365,6 @@
 def on_device(counts, cotangent, saved_gate, saved_up, down_weight):
     tok, ff = saved_gate.shape
     d = cotangent.shape[1]
-    vmem = pl.BlockSpec(memory_space=pltpu.VMEM)
     anywhere = pl.BlockSpec(memory_space=pl.ANY)
     dma = pltpu.SemaphoreType.DMA
     results = pl.pallas_call(
@@ -369,7 +377,7 @@
         in_specs=[
             pl.BlockSpec(memory_space=pltpu.SMEM), anywhere, anywhere, anywhere, anywhere,
         ],
-        out_specs=(vmem, vmem, anywhere),
+        out_specs=(anywhere,) * 3,
         scratch_shapes=[
             pltpu.VMEM((tok, d), jnp.bfloat16),
             pltpu.VMEM((tok, ff), jnp.bfloat16),
@@ -377,9 +385,9 @@
             pltpu.VMEM((ff, d), jnp.bfloat16),
             pltpu.VMEM((GROUPS, tok, d), jnp.bfloat16),
             pltpu.VMEM((GROUPS, ff, tok), jnp.bfloat16),
-            pltpu.VMEM((GROUPS, 2 * TILES, HALF, LANES), jnp.float32),
-            pltpu.VMEM((2, HOPS, 2 * TILES, HALF, LANES), jnp.bfloat16),
-            pltpu.VMEM((2, HOPS, 2 * TILES, HALF, LANES), jnp.bfloat16),
+            pltpu.VMEM((GROUPS, CUTS * TILES, CUT, LANES), jnp.float32),
+            pltpu.VMEM((2, HOPS, CUTS * TILES, CUT, LANES), jnp.bfloat16),
+            pltpu.VMEM((2, HOPS, CUTS * TILES, CUT, LANES), jnp.bfloat16),
             pltpu.VMEM((2, TILES, tok, LANES), jnp.float32),
             pltpu.VMEM((ff, d), jnp.bfloat16),
             dma((4,)), dma, dma((8,)), dma((8,)), dma((8,)), dma((8,)),

time: 119 us -> 116 us (0.975)
  Pallas kernels: 117 us -> 114 us
    pallas_call x1, Pallas kernels: 113 us -> 110 us  [on_device(): pl.pallas_call(kernel, out_shape=(jax.ShapeDtypeStruct((tok, ff), jnp.bfl...]
where the time goes in v5:
time: 116 us; the launch traced here: 115 us
  Pallas kernels  114 us (98%)
    pallas_call x1, Pallas kernels, on_device(): pl.pallas_call(kernel, out_shape=(jax.ShapeDtypeStruct((tok, ff), jnp.bfl...  110 us
    pallas_call x1, Pallas kernels, copied(): pl.pallas_call(functools.partial(copy_kernel, pieces), out_shape=tuple((j...  3.8 us

profile of v5, /device:TPU:32, one launch (start us, length us, event | category | flops | bytes accessed | tf_op | source)
XLA Modules:
  0.0 114.9 jit_solution(10609708400038823827)
XLA Ops:
  0.6 110.4 %down_backward.1 = (bf16[128,1664]{1,0:T(8,128)(2,1)}, bf16[128,1664]{1,0:T(8,128)(2,1)}, bf16[1664,1024]{1,0:T(8,128)(2,1)}) custom-call(s32[16]{0:T(128)} %counts_ref.1, bf16[128,1024]{1,0:T(8,128)(2,1)} %cot_hbm.1, bf16[128,1664]{1,0:T(8,128)(2,1)} %gate_hbm.1, bf16[128,1664]{1,0:T(8,128)(2,1)} %up_hbm.1, bf16[1664,1024]{1,0:T(8,128)(2,1)} %weight_hbm.1), custom_call_target="tpu_custom_call" | custom-call | flops 13958643712 | bytes 8519680 | tf_op jit(solution)/shard_map/down_backward/pallas_call | solution.py:370
  111.1 3.8 %copy_out.1 = (bf16[128,1664]{1,0:T(8,128)(2,1)}, bf16[128,1664]{1,0:T(8,128)(2,1)}, bf16[1664,1024]{1,0:T(8,128)(2,1)}) custom-call(bf16[128,1664]{1,0:T(8,128)(2,1)} %get-tuple-element.6.refs_0_, bf16[128,1664]{1,0:T(8,128)(2,1)} %get-tuple-element.7.refs_1_, bf16[1664,1024]{1,0:T(8,128)(2,1)} %get-tuple-element.8.refs_2_), custom_call_target="tpu_custom_call" | custom-call | tf_op jit(solution)/shard_map/copy_out/pallas_call | solution.py:354
